TPU v7x, 32 devices: a whole 2x2x4 slice. The times are simulated.
32 devices in a mesh: grp: 2 (over x), dev: 16 (over z, y, core).
Axes of the slice: x: 2, y: 2, z: 4, core: 2. Of those that a mesh axis runs over, the one named last changes fastest.
Arguments:
- frames: bfloat16 [80, 64, 1408], P('dev'), may hold values from -100 to 100
- trained: int32 [80], replicated, may hold values from 0 to 3071, as said below
- frame_of: int32 [6144], P('dev'), may hold values from 0 to 3071, as said below
- token_cache: bfloat16 [6144, 1408], P('dev'), may hold values from -100 to 100
- norm_gains: float32 [2, 1408], P('grp'), may hold values from 0.1 to 1.9
- proj_weights: bfloat16 [2, 1408, 4224], P('grp'), may hold values from -4 to 4
- out_weights: bfloat16 [2, 1408, 1408], P('grp'), may hold values from -0.15625 to 0.15625
- patch_cotangent: bfloat16 [80, 64, 1408], P('dev'), may hold values from -0.119628906 to 0.119628906
- time_cotangent: bfloat16 [6144, 1408], P('dev'), may hold values from -6 to 6
Outputs:
- weight_grad: float32 [2, 1408, 1408], P('grp', 'dev')
Inputs may be any that keep to these rules, and one draw needn't show every extreme that they name: `trained`: 80 different frames of the video; among them, for every k, the frames k * 192 and (k + 1) * 192 - 1. `frame_of`: never falls along the tokens; tokens 4 m to 4 m + 3 belong to frames 2 m and 2 m + 1, each frame having 1 to 3 tokens.
All inputs are finite; a program needn't handle non-finite values.
Results may differ from a plain program's by a relative error of at most 0.0078.
Values may be sent and summed in bfloat16 or wider, within the bound.
A program may use at most 192 MiB of HBM per device.

v0:
```python
import jax
import jax.numpy as jnp
from jax import lax
from jax.sharding import PartitionSpec as P

HEADS = 16
HEAD_DIM = 88
SPAN = 128
EPS = 1e-06
HIGH_PRECISION = lax.Precision.HIGHEST


def from_behind(value, axis, steps):
    count = lax.axis_size(axis)
    initial, last = (max(0, -steps), min(count, count - steps))
    return lax.ppermute(value, axis, [(source, source + steps) for source in range(initial, last)])


def with_halo(array, sides, width):
    for axis, dim in sides:
        size, length = (lax.axis_size(axis), array.shape[dim])
        up = [(i, (i + 1) % size) for i in range(size - 1)]
        down = [(j, i) for i, j in up]
        last = lax.slice_in_dim(array, length - width, length, axis=dim)
        initial = lax.slice_in_dim(array, 0, width, axis=dim)
        before = lax.ppermute(last, axis, up)
        after = lax.ppermute(initial, axis, down)
        array = jnp.concatenate([before, array, after], axis=dim)
    return array


def normalize(rows):
    inverse = lax.rsqrt(jnp.mean(rows * rows, axis=-1, keepdims=True) + EPS)
    return (rows * inverse, inverse)


def when_true(flag, compute):

    def skipped():
        return jax.tree.map(jnp.zeros_like, compute())

    return lax.cond(flag, compute, skipped)


def contract_rows(left, right):
    return lax.dot_general(
        left, right, (((0,), (0,)), ((), ())), preferred_element_type=jnp.float32
    )


def contract_exact(left, right):
    return lax.dot_general(left, right, (((0,), (0,)), ((), ())), precision=HIGH_PRECISION)


def contract_cols(left, right):
    return lax.dot_general(
        left, right, (((1,), (1,)), ((), ())), preferred_element_type=jnp.float32
    )


def stack_windows(extended, count):
    return jnp.stack([extended[block * SPAN : (block + 3) * SPAN] for block in range(count)])


def shards(
    frames,
    trained,
    frame_of,
    token_cache,
    norm_gains,
    proj_weights,
    out_weights,
    patch_cotangent,
    time_cotangent,
):
    spatial = lax.axis_index("grp") == 0
    temporal = jnp.logical_not(spatial)
    norm_gain = norm_gains[0]
    in_proj = proj_weights[0]
    out_proj = out_weights[0]
    width = in_proj.shape[0]
    frame_count, patches, _ = frames.shape
    token_count = token_cache.shape[0]
    nblocks = token_count // SPAN
    score_scale = HEAD_DIM ** (-0.5)
    first_token = lax.axis_index("dev") * token_count
    token_total = lax.axis_size("dev") * token_count
    win_pos = (
        first_token
        + (jnp.arange(nblocks, dtype=jnp.int32)[:, None] - 1) * SPAN
        + jnp.arange(3 * SPAN, dtype=jnp.int32)[None, :]
    )
    win_valid = (win_pos >= 0) & (win_pos < token_total)

    def spatial_forward():
        rows = frames.reshape(frame_count * patches, width).astype(jnp.float32)
        scaled_rows, _ = normalize(rows)
        normed = (scaled_rows * norm_gain).astype(jnp.bfloat16)
        packed = jnp.dot(normed, in_proj, preferred_element_type=jnp.float32).astype(jnp.bfloat16)
        packed = packed.reshape(frame_count, patches, 3, HEADS, HEAD_DIM)
        attention_logits = (
            jnp.einsum(
                "fphd,fqhd->fhpq",
                packed[:, :, 0],
                packed[:, :, 1],
                preferred_element_type=jnp.float32,
            )
            * score_scale
        )
        attention_probs = jax.nn.softmax(attention_logits, axis=-1).astype(jnp.bfloat16)
        attended_output = jnp.einsum(
            "fhpq,fqhd->fphd", attention_probs, packed[:, :, 2], preferred_element_type=jnp.float32
        )
        attended_output = attended_output.astype(jnp.bfloat16).reshape(frame_count * patches, width)
        output = rows + jnp.dot(attended_output, out_proj, preferred_element_type=jnp.float32)
        pooled = jnp.mean(output.reshape(frame_count, patches, width), axis=1).astype(jnp.bfloat16)
        return (pooled, attended_output)

    pooled, spatial_mixed = when_true(spatial, spatial_forward)
    handed = from_behind(pooled, "grp", 1)
    arrived = lax.all_gather(handed, "dev", axis=0, tiled=True)

    def temporal_front():
        selector = (frame_of[:, None] == trained[None, :]).astype(jnp.bfloat16)
        inputs = token_cache.astype(jnp.float32) + jnp.dot(
            selector, arrived, preferred_element_type=jnp.float32
        )
        scaled_rows, inverse = normalize(inputs)
        normed = (scaled_rows * norm_gain).astype(jnp.bfloat16)
        packed = jnp.dot(normed, in_proj, preferred_element_type=jnp.float32).astype(jnp.bfloat16)
        return (selector, scaled_rows, inverse, packed[:, :width], packed[:, width:])

    selector, scaled_rows, inverse, queries, key_value = when_true(temporal, temporal_front)
    extended = with_halo(key_value, (("dev", 0),), SPAN)
    key_window = stack_windows(extended, nblocks)
    key_heads = key_window[..., :width].reshape(nblocks, 3 * SPAN, HEADS, HEAD_DIM)
    value_heads = key_window[..., width:].reshape(nblocks, 3 * SPAN, HEADS, HEAD_DIM)
    query_heads = queries.reshape(nblocks, SPAN, HEADS, HEAD_DIM)

    def temporal_attend():
        attention_logits = (
            jnp.einsum(
                "bqhd,bkhd->bhqk", query_heads, key_heads, preferred_element_type=jnp.float32
            )
            * score_scale
        )
        attention_logits = jnp.where(win_valid[:, None, None, :], attention_logits, -1e30)
        row_top = jnp.max(attention_logits, axis=-1, keepdims=True)
        log_total = row_top + jnp.log(
            jnp.sum(jnp.exp(attention_logits - row_top), axis=-1, keepdims=True)
        )
        chances = jnp.exp(attention_logits - log_total)
        chance_weights = chances.astype(jnp.bfloat16)
        attended_output = jnp.einsum(
            "bhqk,bkhd->bqhd", chance_weights, value_heads, preferred_element_type=jnp.float32
        )
        return (
            chances,
            chance_weights,
            log_total[..., 0],
            attended_output.astype(jnp.bfloat16).reshape(token_count, width),
        )

    chances, chance_weights, log_total, time_mixed = when_true(temporal, temporal_attend)

    def temporal_grads():
        grad_mixed = contract_cols(time_cotangent, out_proj).astype(jnp.bfloat16)
        grad_heads = grad_mixed.reshape(nblocks, SPAN, HEADS, HEAD_DIM)
        mixed_heads = time_mixed.reshape(nblocks, SPAN, HEADS, HEAD_DIM)
        row_delta = jnp.sum(
            grad_heads.astype(jnp.float32) * mixed_heads.astype(jnp.float32), axis=-1
        ).transpose(0, 2, 1)
        probability_gradient = jnp.einsum(
            "bqhd,bkhd->bhqk", grad_heads, value_heads, preferred_element_type=jnp.float32
        )
        logit_gradient = (chances * (probability_gradient - row_delta[..., None])).astype(
            jnp.bfloat16
        )
        query_gradient = (
            jnp.einsum(
                "bhqk,bkhd->bqhd", logit_gradient, key_heads, preferred_element_type=jnp.float32
            )
            * score_scale
        )
        return (grad_mixed, row_delta, logit_gradient, query_gradient.reshape(token_count, width))

    grad_mixed, row_delta, logit_gradient, query_gradient = when_true(temporal, temporal_grads)
    stats = jnp.concatenate(
        [
            log_total.transpose(0, 2, 1).reshape(token_count, HEADS),
            row_delta.transpose(0, 2, 1).reshape(token_count, HEADS),
        ],
        axis=-1,
    )
    near_stats = with_halo(stats, (("dev", 0),), SPAN)
    near_rows = with_halo(jnp.concatenate([queries, grad_mixed], axis=-1), (("dev", 0),), SPAN)

    def rim_keys():
        row_window = stack_windows(near_rows, nblocks)
        stat_window = stack_windows(near_stats, nblocks)
        query_part = row_window[..., :width].reshape(nblocks, 3 * SPAN, HEADS, HEAD_DIM)
        grad_part = row_window[..., width:].reshape(nblocks, 3 * SPAN, HEADS, HEAD_DIM)
        totals = stat_window[..., :HEADS].transpose(0, 2, 1)
        deltas = stat_window[..., HEADS:].transpose(0, 2, 1)
        own_keys = key_value[:, :width].reshape(nblocks, SPAN, HEADS, HEAD_DIM)
        own_values = key_value[:, width:].reshape(nblocks, SPAN, HEADS, HEAD_DIM)
        attention_logits = (
            jnp.einsum("bqhd,bkhd->bhqk", query_part, own_keys, preferred_element_type=jnp.float32)
            * score_scale
        )
        again = jnp.where(
            win_valid[:, None, :, None],
            jnp.exp(
                jnp.where(win_valid[:, None, :, None], attention_logits - totals[..., None], 0.0)
            ),
            0.0,
        )
        probability_gradient = jnp.einsum(
            "bqhd,bkhd->bhqk", grad_part, own_values, preferred_element_type=jnp.float32
        )
        part_score = (again * (probability_gradient - deltas[..., None])).astype(jnp.bfloat16)
        key_gradient = (
            jnp.einsum(
                "bhqk,bqhd->bkhd", part_score, query_part, preferred_element_type=jnp.float32
            )
            * score_scale
        )
        value_gradient = jnp.einsum(
            "bhqk,bqhd->bkhd",
            again.astype(jnp.bfloat16),
            grad_part,
            preferred_element_type=jnp.float32,
        )
        return jnp.concatenate(
            [key_gradient.reshape(token_count, width), value_gradient.reshape(token_count, width)],
            axis=-1,
        )

    key_grads = when_true(temporal, rim_keys)

    def temporal_back():
        grad_packed = jnp.concatenate([query_gradient, key_grads], axis=-1).astype(jnp.bfloat16)
        grad_scaled = contract_cols(grad_packed, in_proj) * norm_gain
        grad_inputs = inverse * (
            grad_scaled - scaled_rows * jnp.mean(grad_scaled * scaled_rows, axis=-1, keepdims=True)
        ) + time_cotangent.astype(jnp.float32)
        return contract_exact(selector.astype(jnp.float32), grad_inputs)

    frame_grads = when_true(temporal, temporal_back)
    reduced = lax.psum_scatter(frame_grads, "dev", scatter_dimension=0, tiled=True)
    returned = from_behind(reduced, "grp", -1)

    def spatial_right():
        grads = patch_cotangent.astype(jnp.float32) + returned[:, None, :] / patches
        return grads.reshape(frame_count * patches, width)

    right_side = when_true(spatial, spatial_right)

    def from_frames():
        return contract_exact(spatial_mixed.astype(jnp.float32), right_side)

    def from_tokens():
        return contract_rows(time_mixed, time_cotangent)

    weight_part = lax.psum_scatter(
        lax.cond(spatial, from_frames, from_tokens), "dev", scatter_dimension=0, tiled=True
    )
    return weight_part[None]


def solution(mesh):
    in_specs = (
        P("dev", None, None),
        P(),
        P("dev"),
        P("dev", None),
        P("grp", None),
        P("grp", None, None),
        P("grp", None, None),
        P("dev", None, None),
        P("dev", None),
    )
    out_specs = P("grp", "dev", None)
    return jax.shard_map(shards, mesh=mesh, in_specs=in_specs, out_specs=out_specs, check_vma=False)
```

profile of v0, /device:TPU:0, one launch (start us, length us, event | category | flops | bytes accessed | tf_op | source)
XLA Modules:
  0.0 491.3 jit_solution(10621586428022382250)
XLA Ops:
  6.5 40.0 %conditional.8 = (bf16[5,1408]{1,0:T(8,128)(2,1)S(1)}, bf16[320,1408]{1,0:T(8,128)(2,1)}) conditional(s32[]{:T(128)} %convert_element_type.90, () %tuple.65, (bf16[5,64,1408]{2,1,0:T(8,128)(2,1)}, f32[1,1408]{1,0:T(1,128)}, bf16[1408,4224]{1,0:T(8,128)(2,1)}, bf16[1408,1408]{1,0:T(8,128)(2,1)}) %tuple.143), branch_computations={%region_0.0_spmd, %region_1.0_spmd} | conditional | flops 5198732288 | bytes 54580020 | solution.py:42
  6.5 1.5 multiply_reduce_fusion.2
  8.1 0.7 reduce.1
  8.8 1.4 fusion.44
  10.3 9.1 %convolution_convert_fusion.1 = bf16[320,4224]{1,0:T(8,128)(2,1)S(1)} fusion(bf16[320,1408]{1,0:T(8,128)(2,1)S(1)} %fusion.44, bf16[1408,4224]{1,0:T(8,128)(2,1)} %get-tuple-element.100), kind=kOutput, calls=%fused_computation.55 | convolution fusion | flops 3807682560 | bytes 15499264 | tf_op jit(solution)/shard_map/cond/branch_1_fun/dot_general | solution.py:99
  19.4 8.5 %reshape.116 = bf16[5,64,3,16,88]{4,3,2,1,0:T(8,128)(2,1)} reshape(bf16[320,4224]{1,0:T(8,128)(2,1)S(1)} %convolution_convert_fusion.1) | data formatting | bytes 5406720 | tf_op jit(solution)/shard_map/cond/branch_1_fun/reshape | solution.py:100
  27.9 3.0 fusion.76
  31.0 0.8 fusion.46
  31.8 3.9 fusion.77
  35.7 0.8 fusion.45
  36.5 0.9 copy.58
  37.4 2.2 reshape.117
  39.6 5.3 %convolution_add_fusion = f32[320,1408]{1,0:T(8,128)} fusion(bf16[320,1408]{1,0:T(8,128)(2,1)} %reshape.117, bf16[1408,1408]{1,0:T(8,128)(2,1)} %get-tuple-element.101, bf16[320,1408]{1,0:T(8,128)(2,1)S(1)} %bitcast.144), kind=kOutput, calls=%fused_computation.56 | convolution fusion | flops 1269678080 | bytes 7569408 | tf_op jit(solution)/shard_map/cond/branch_1_fun/dot_general | solution.py:115
  44.9 1.6 reduce_sum.58
  46.5 1.3 collective-permute-start
  47.8 1.5 collective-permute-done
  49.3 24.1 %all-gather = bf16[16,5,1408]{2,1,0:T(8,128)(2,1)S(1)} all-gather(bf16[1,5,1408]{2,1,0:T(8,128)(2,1)S(1)} %bitcast.152), channel_id=1, replica_groups=mesh['grp'=2,'dev'=16] {'dev'}, dimensions={0}, use_global_device_ids=true | all-gather | bytes 239360 | tf_op jit(solution)/shard_map/all_gather | solution.py:121
  73.4 0.1 reshape.142
  73.5 4.5 conditional.9
  73.6 1.5 broadcast.148
  75.1 0.1 broadcast.151
  75.2 1.5 reshape.119
  76.7 1.1 broadcast.150.clone
  78.0 1.3 copy-done.2
  79.4 2.9 copy.69
  82.3 1.0 fusion.80
  83.3 3.1 collective-permute-start.1
  86.4 1.3 collective-permute-start.2
  87.7 2.3 constant_dynamic-update-slice_fusion.1
  90.1 0.5 collective-permute-done.2
  90.6 1.8 fusion.70
  92.4 1.3 pad_maximum_fusion.3
  93.7 0.7 fusion.78
  94.3 1.7 copy-done
  96.0 6.1 %conditional.10 = (f32[3,16,128,384]{3,2,1,0:T(8,128)}, f32[3,16,128]{2,1,0:T(8,128)S(1)}, bf16[384,1408]{0,1:T(8,128)(2,1)}) conditional(s32[]{:T(128)} %convert_element_type.91, () %tuple.63, (pred[3,384]{1,0:T(4,128)(4,1)S(1)}, bf16[3,128,16,88]{1,0,3,2:T(4,128)(2,1)}, bf16[3,384,16,88]{1,3,2,0:T(8,128)(2,1)S(1)}, ...), branch_computations={%region_9.0_spmd, %region_10.13_spmd} | conditional | flops 856958976 | bytes 60534224 | solution.py:42
  96.0 4.8 broadcast.154
  100.8 1.1 broadcast.156
  102.1 6.0 %conditional.11 = (f32[3,16,128]{2,0,1:T(4,128)S(1)}, bf16[384,1408]{0,1:T(8,128)(2,1)}, bf16[384,1408]{0,1:T(8,128)(2,1)}) conditional(s32[]{:T(128)} %convert_element_type.91, () %tuple.72, (bf16[384,1408]{1,0:T(8,128)(2,1)}, bf16[1408,1408]{1,0:T(8,128)(2,1)}, bf16[384,1408]{0,1:T(8,128)(2,1)}, bf16[3,384,16,88]{1,3,2,0:T(8,128)(2,1)}, ...), branch_computations={%region_13.14_spmd, %region_14.16_spmd} | conditional | flops 2363320320 | bytes 39649360 | solution.py:42
  102.1 1.1 broadcast.158.clone
  103.2 1.1 broadcast.160
  108.0 2.3 constant_dynamic-update-slice_fusion
  110.4 1.6 fusion.79
  111.9 13.2 %collective-permute-start.3 = (bf16[128,2816]{0,1:T(8,128)(2,1)S(1)}, bf16[128,2816]{0,1:T(8,128)(2,1)S(1)}, u32[]{:S(2)}, u32[]{:S(2)}) collective-permute-start(bf16[128,2816]{0,1:T(8,128)(2,1)S(1)} %get-tuple-element.261), channel_id=1, source_target_pairs={{0,1},{1,2},{2,3},{3,4},{4,5},{5,6},{6,7},{7,8},{8,9},{9,10},{10,1... | collective-permute-start | bytes 2162696 | tf_op jit(solution)/shard_map/ppermute | solution.py:26
  125.1 1.3 collective-permute-start.4
  126.5 5.0 %collective-permute-start.5 = (f32[128,32]{0,1:T(8,128)S(1)}, f32[128,32]{0,1:T(8,128)S(1)}, u32[]{:S(2)}, u32[]{:S(2)}) collective-permute-start(f32[128,32]{0,1:T(8,128)S(1)} %get-tuple-element.267), channel_id=1, source_target_pairs={{0,1},{1,2},{2,3},{3,4},{4,5},{5,6},{6,7},{7,8},{8,9},{9,10},{10,1... | collective-permute-start | bytes 49160 | tf_op jit(solution)/shard_map/ppermute | solution.py:26
  131.4 1.3 collective-permute-start.6
  132.7 3.0 collective-permute-done.6
  135.8 2.1 pad_maximum_fusion.4
  137.9 0.4 copy-done.3
  138.3 0.7 conditional.12
  138.3 0.2 broadcast.162
  139.0 8.4 %conditional.13 = (f32[80,1408]{1,0:T(8,128)}) conditional(s32[]{:T(128)} %convert_element_type.91, () %tuple.71, (f32[384,1]{0,1:T(1,128)S(1)}, bf16[384,1408]{0,1:T(8,128)(2,1)}, bf16[384,2816]{0,1:T(8,128)(2,1)S(1)}, bf16[1408,4224]{1,0:T(8,128)(2,1)}, f32[1,1408]{1,0:T(1,128)}, /*index=5*/f32[384,1408]{1,0:T(8,128)}, ...), branch_computations={%region_18.19_spmd, %region_19.21_spmd} | conditional | flops 5097455616 | bytes 36246600 | solution.py:42
  139.0 0.8 broadcast.165
  147.5 0.6 dynamic-slice
  148.7 213.6 %all-reduce.4.cloned.1.call-done = f32[80,1408]{1,0:T(8,128)} async-done(((f32[80,1408]{1,0:T(8,128)}), f32[80,1408]{1,0:T(8,128)}) %all-reduce.4.cloned.1.call-update) | async-done | bytes 450576
  362.3 0.9 constant_dynamic-slice_fusion
  363.2 1.3 collective-permute-start.7
  364.5 4.7 collective-permute-done.7
  369.1 1.4 conditional.14
  369.1 1.4 convert_add_fusion
  370.5 0.1 copy-done.5
  370.6 10.3 %conditional.15 = (f32[1408,1408]{1,0:T(8,128)}) conditional(s32[]{:T(128)} %convert_element_type.90, (bf16[384,1408]{0,1:T(8,128)(2,1)}, bf16[384,1408]{1,0:T(8,128)(2,1)S(1)}) %tuple.137, (bf16[320,1408]{1,0:T(8,128)(2,1)}, f32[320,1408]{1,0:T(8,128)S(1)}) %tuple.78), branch_computations={%region_24.25_spmd, %region_25.26_spmd} | conditional | flops 7612661760 | bytes 10633224 | solution.py:266
  370.6 10.3 %fusion.83 = f32[1408,1408]{1,0:T(8,128)} fusion(bf16[320,1408]{1,0:T(8,128)(2,1)} %get-tuple-element.136, f32[320,1408]{1,0:T(8,128)S(1)} %get-tuple-element.137), kind=kOutput, calls=%fused_computation.129 | convolution fusion | flops 7612661760 | bytes 10633216 | tf_op jit(solution)/shard_map/cond/branch_1_fun/dot_general | solution.py:52
  381.0 103.3 %reduce-scatter.4.cloned.1.call-done = f32[88,1408]{1,0:T(8,128)} async-done(((f32[1408,1408]{1,0:T(8,128)}), f32[88,1408]{1,0:T(8,128)}) %reduce-scatter.4.cloned.1.call-update) | async-done | bytes 495632
  (36 shorter events, 0.3 us)
Async XLA Ops:
  6.5 355.7 %all-reduce.4.cloned.1.call-start = ((), (), s32[]{:S(2)}) async-start(), calls=%async_computation.1 | async-start | bytes 901120
  6.5 67.0 %copy-start.15 = (s32[384]{0:T(512)S(1)}, s32[384]{0:T(512)}, u32[]{:S(2)}) copy-start(s32[384]{0:T(512)} %param.27) | copy-start | bytes 4612
  6.5 67.0 %copy-start.16 = (s32[80]{0:T(128)S(1)}, s32[80]{0:T(128)}, u32[]{:S(2)}) copy-start(s32[80]{0:T(128)} %param.26) | copy-start | bytes 964
  36.5 3.1 copy-start.7
  46.5 2.8 collective-permute-start
  78.0 1.3 copy-start.2
  83.3 6.8 %collective-permute-start.1 = (bf16[128,2816]{0,1:T(8,128)(2,1)}, bf16[128,2816]{0,1:T(8,128)(2,1)}, u32[]{:S(2)}, u32[]{:S(2)}) collective-permute-start(bf16[128,2816]{0,1:T(8,128)(2,1)} %get-tuple-element.265), channel_id=1, source_target_pairs={{0,1},{1,2},{2,3},{3,4},{4,5},{5,6},{6,7},{7,8},{8,9},{9,10},{10,1... | collective-permute-start | bytes 2162696 | tf_op jit(solution)/shard_map/ppermute | solution.py:26
  86.4 4.2 collective-permute-start.2
  94.3 1.7 copy-start
  110.4 25.4 %copy-start.1 = (bf16[384,2816]{0,1:T(8,128)(2,1)S(1)}, bf16[384,2816]{0,1:T(8,128)(2,1)}, u32[]{:S(2)}) copy-start(bf16[384,2816]{0,1:T(8,128)(2,1)} %constant_dynamic-update-slice_fusion) | copy-start | bytes 6488068
  111.9 23.8 %collective-permute-start.3 = (bf16[128,2816]{0,1:T(8,128)(2,1)S(1)}, bf16[128,2816]{0,1:T(8,128)(2,1)S(1)}, u32[]{:S(2)}, u32[]{:S(2)}) collective-permute-start(bf16[128,2816]{0,1:T(8,128)(2,1)S(1)} %get-tuple-element.261), channel_id=1, source_target_pairs={{0,1},{1,2},{2,3},{3,4},{4,5},{5,6},{6,7},{7,8},{8,9},{9,10},{10,1... | collective-permute-start | bytes 2162696 | tf_op jit(solution)/shard_map/ppermute | solution.py:26
  125.1 10.7 %collective-permute-start.4 = (bf16[128,2816]{0,1:T(8,128)(2,1)S(1)}, bf16[128,2816]{0,1:T(8,128)(2,1)S(1)}, u32[]{:S(2)}, u32[]{:S(2)}) collective-permute-start(bf16[128,2816]{0,1:T(8,128)(2,1)S(1)} %get-tuple-element.262), channel_id=1, source_target_pairs={{1,0},{2,1},{3,2},{4,3},{5,4},{6,5},{7,6},{8,7},{9,8},{10,9},{11,1... | collective-permute-start | bytes 2162696 | tf_op jit(solution)/shard_map/ppermute | solution.py:27
  126.5 6.3 %collective-permute-start.5 = (f32[128,32]{0,1:T(8,128)S(1)}, f32[128,32]{0,1:T(8,128)S(1)}, u32[]{:S(2)}, u32[]{:S(2)}) collective-permute-start(f32[128,32]{0,1:T(8,128)S(1)} %get-tuple-element.267), channel_id=1, source_target_pairs={{0,1},{1,2},{2,3},{3,4},{4,5},{5,6},{6,7},{7,8},{8,9},{9,10},{10,1... | collective-permute-start | bytes 49160 | tf_op jit(solution)/shard_map/ppermute | solution.py:26
  131.4 4.3 collective-permute-start.6
  135.8 2.6 copy-start.3
  139.0 8.5 %copy-start.17 = (u32[32]{0:T(128)S(1)}, u32[32]{0:T(128)}, u32[]{:S(2)}) copy-start(u32[32]{0:T(128)} %constant.101) | copy-start | bytes 388
  147.5 336.8 %reduce-scatter.4.cloned.1.call-start = ((), (), s32[]{:S(2)}) async-start(), calls=%async_computation.2 | async-start | bytes 8425472
  363.2 6.0 %collective-permute-start.7 = (f32[5,1408]{1,0:T(8,128)S(1)}, f32[5,1408]{1,0:T(8,128)S(1)}, u32[]{:S(2)}, u32[]{:S(2)}) collective-permute-start(f32[5,1408]{1,0:T(8,128)S(1)} %constant_dynamic-slice_fusion), channel_id=1, source_target_pairs={{16,0},{17,1},{18,2},{19,3},{20,4},{21,5},{22,6},{23,7},{24,8},{25... | collective-permute-start | bytes 84488 | tf_op jit(solution)/shard_map/ppermute | solution.py:16
  369.1 1.5 copy-start.5
Sparse Core Ops, SparseCore 0:
  147.6 214.6 all-reduce.3
  381.1 103.1 reduce-scatter.3
where the time goes:
time: 500 us; the launch traced here: 491 us
  waiting for transfers between devices  327 us (65%)
  local copies, waits for them, and re-layouts  44.1 us (9%)
  starting transfers between devices  27.7 us (6%)
  matrix products  26.3 us (5%)
  blocking collectives  24.1 us (5%)
  other arithmetic  15.8 us (3%)
  between operations  14.4 us (3%)
  loops' own time  12.3 us (2%)
    unnamed x4, waiting for transfers between devices  317 us
    all_gather x1, blocking collectives, shards(): arrived = lax.all_gather(handed, 'dev', axis=0, tiled=True)  24.1 us
    ppermute x3, starting transfers between devices, with_halo(): before = lax.ppermute(last, axis, up)  21.2 us
    another operation x7, loops' own time, when_true(): return lax.cond(flag, compute, skipped)  12.3 us
    another operation x13, local copies, waits for them, and re-layouts  11.9 us
    dot_general x1, matrix products, contract_exact(): lax.dot_general(left, right, (((0,), (0,)), ((), ())), precision=HIGH_PRE...  10.3 us
  transfers between devices with their start and end apart: 10, of which 6 were waited for; matrix products, arithmetic and copies ran while one was open for 1% of the time, Pallas kernels for 0%

commit v1 on v0

--- a/solution.py
+++ b/solution.py
@@ -8,6 +8,18 @@
 SPAN = 128
 EPS = 1e-06
 HIGH_PRECISION = lax.Precision.HIGHEST
+
+
+def doubled_up(x, axis, dim):
+    ways, here, step = (lax.axis_size(axis), lax.axis_index(axis), x.shape[dim])
+    line, have = (x, 1)
+    while have < ways:
+        line = jnp.concatenate(
+            [line, lax.ppermute(line, axis, [(d, (d - have) % ways) for d in range(ways)])],
+            axis=dim,
+        )
+        have = 2 * have
+    return jnp.roll(line, here * step, axis=dim)
 
 
 def from_behind(value, axis, steps):
@@ -118,7 +130,7 @@
 
     pooled, spatial_mixed = when_true(spatial, spatial_forward)
     handed = from_behind(pooled, "grp", 1)
-    arrived = lax.all_gather(handed, "dev", axis=0, tiled=True)
+    arrived = doubled_up(handed, "dev", 0)
 
     def temporal_front():
         selector = (frame_of[:, None] == trained[None, :]).astype(jnp.bfloat16)

time: 500 us -> 503 us (level)
  blocking collectives: 24.1 us -> 0 us
  waiting for transfers between devices: 327 us -> 344 us
  starting transfers between devices: 27.7 us -> 36 us
    all_gather x1 -> x0, blocking collectives: 24.1 us -> none  [shards(): arrived = lax.all_gather(handed, 'dev', axis=0, tiled=True)]
    ppermute x0 -> x4, waiting for transfers between devices: none -> 16.8 us  [doubled_up(): lax.ppermute(line, axis, [(d, (d - have) % ways) for d in range(ways)])]
    ppermute x0 -> x4, starting transfers between devices: none -> 6.63 us  [doubled_up(): lax.ppermute(line, axis, [(d, (d - have) % ways) for d in range(ways)])]
  transfers between devices with their start and end apart: 10 -> 14, of which waited for: 6 -> 10; matrix products, arithmetic and copies ran while one was open for 1% -> 1% of each run, Pallas kernels for 0% -> 0%
where the time goes in v1:
time: 503 us; the launch traced here: 494 us
  waiting for transfers between devices  344 us (68%)
  local copies, waits for them, and re-layouts  45.2 us (9%)
  starting transfers between devices  36 us (7%)
  matrix products  26.3 us (5%)
  other arithmetic  15.9 us (3%)
  between operations  14.6 us (3%)
  loops' own time  12.3 us (2%)
    unnamed x4, waiting for transfers between devices  319 us
    ppermute x3, starting transfers between devices, with_halo(): before = lax.ppermute(last, axis, up)  22.9 us
    ppermute x4, waiting for transfers between devices, doubled_up(): lax.ppermute(line, axis, [(d, (d - have) % ways) for d in range(ways)])  16.8 us
    another operation x7, loops' own time, when_true(): return lax.cond(flag, compute, skipped)  12.3 us
    another operation x13, local copies, waits for them, and re-layouts  11.9 us
    dot_general x1, matrix products, contract_exact(): lax.dot_general(left, right, (((0,), (0,)), ((), ())), precision=HIGH_PRE...  10.2 us
  transfers between devices with their start and end apart: 14, of which 10 were waited for; matrix products, arithmetic and copies ran while one was open for 1% of the time, Pallas kernels for 0%

profile of v1, /device:TPU:0, one launch (start us, length us, event | category | flops | bytes accessed | tf_op | source)
XLA Modules:
  0.0 494.0 jit_solution(272811089425823720)
XLA Ops:
  6.5 40.0 %conditional.8 = (bf16[5,1408]{1,0:T(8,128)(2,1)S(1)}, bf16[320,1408]{1,0:T(8,128)(2,1)}) conditional(s32[]{:T(128)} %convert_element_type.90, () %tuple.65, (bf16[5,64,1408]{2,1,0:T(8,128)(2,1)}, f32[1,1408]{1,0:T(1,128)}, bf16[1408,4224]{1,0:T(8,128)(2,1)}, bf16[1408,1408]{1,0:T(8,128)(2,1)}) %tuple.146), branch_computations={%region_0.0_spmd, %region_1.0_spmd} | conditional | flops 5198732288 | bytes 54580020 | solution.py:54
  6.5 1.5 multiply_reduce_fusion.2
  8.1 0.7 reduce.1
  8.8 1.4 fusion.44
  10.3 9.1 %convolution_convert_fusion.1 = bf16[320,4224]{1,0:T(8,128)(2,1)S(1)} fusion(bf16[320,1408]{1,0:T(8,128)(2,1)S(1)} %fusion.44, bf16[1408,4224]{1,0:T(8,128)(2,1)} %get-tuple-element.100), kind=kOutput, calls=%fused_computation.55 | convolution fusion | flops 3807682560 | bytes 15499264 | tf_op jit(solution)/shard_map/cond/branch_1_fun/dot_general | solution.py:111
  19.4 8.5 %reshape.116 = bf16[5,64,3,16,88]{4,3,2,1,0:T(8,128)(2,1)} reshape(bf16[320,4224]{1,0:T(8,128)(2,1)S(1)} %convolution_convert_fusion.1) | data formatting | bytes 5406720 | tf_op jit(solution)/shard_map/cond/branch_1_fun/reshape | solution.py:112
  27.9 3.0 fusion.78
  30.9 0.8 fusion.46
  31.8 3.9 fusion.79
  35.7 0.8 fusion.45
  36.5 0.9 copy.61
  37.3 2.2 reshape.117
  39.6 5.3 %convolution_add_fusion = f32[320,1408]{1,0:T(8,128)} fusion(bf16[320,1408]{1,0:T(8,128)(2,1)} %reshape.117, bf16[1408,1408]{1,0:T(8,128)(2,1)} %get-tuple-element.101, bf16[320,1408]{1,0:T(8,128)(2,1)S(1)} %bitcast.142), kind=kOutput, calls=%fused_computation.56 | convolution fusion | flops 1269678080 | bytes 7569408 | tf_op jit(solution)/shard_map/cond/branch_1_fun/dot_general | solution.py:127
  44.9 1.6 reduce_sum.58
  46.5 1.3 collective-permute-start
  47.8 1.5 collective-permute-done
  49.3 4.9 collective-permute-start.1
  54.2 1.5 collective-permute-done.1
  55.7 1.2 collective-permute-start.2
  56.9 2.9 collective-permute-done.2
  60.4 3.9 collective-permute-done.3
  64.5 8.5 %collective-permute-done.4 = bf16[40,1408]{1,0:T(8,128)(2,1)S(1)} collective-permute-done((bf16[40,1408]{1,0:T(8,128)(2,1)S(1)}, bf16[40,1408]{1,0:T(8,128)(2,1)S(1)}, u32[]{:S(2)}, u32[]{:S(2)}) %collective-permute-start.4) | collective-permute-done | bytes 112672 | tf_op jit(solution)/shard_map/ppermute | solution.py:18
  72.9 1.1 concatenate.47
  74.1 4.5 conditional.9
  74.1 1.6 broadcast.148
  75.8 1.5 reshape.119
  77.3 1.1 broadcast.150.clone
  78.6 1.3 copy-done.2
  80.0 2.9 copy.72
  82.9 1.0 fusion.82
  83.8 2.8 collective-permute-start.5
  86.7 1.3 collective-permute-start.6
  88.0 2.3 constant_dynamic-update-slice_fusion.1
  90.4 1.2 collective-permute-done.6
  91.6 1.8 fusion.72
  93.4 1.3 pad_maximum_fusion.3
  94.7 0.7 fusion.80
  95.4 1.7 copy-done
  97.1 6.1 %conditional.10 = (f32[3,16,128,384]{3,2,1,0:T(8,128)}, f32[3,16,128]{2,1,0:T(8,128)S(1)}, bf16[384,1408]{0,1:T(8,128)(2,1)}) conditional(s32[]{:T(128)} %convert_element_type.91, () %tuple.63, (pred[3,384]{1,0:T(4,128)(4,1)S(1)}, bf16[3,128,16,88]{1,0,3,2:T(4,128)(2,1)}, bf16[3,384,16,88]{1,3,2,0:T(8,128)(2,1)S(1)}, ...), branch_computations={%region_9.10_spmd, %region_10.13_spmd} | conditional | flops 856958976 | bytes 60534224 | solution.py:54
  97.1 4.8 broadcast.154
  101.9 1.1 broadcast.156
  103.2 6.0 %conditional.11 = (f32[3,16,128]{2,0,1:T(4,128)S(1)}, bf16[384,1408]{0,1:T(8,128)(2,1)}, bf16[384,1408]{0,1:T(8,128)(2,1)}) conditional(s32[]{:T(128)} %convert_element_type.91, () %tuple.72, (bf16[384,1408]{1,0:T(8,128)(2,1)}, bf16[1408,1408]{1,0:T(8,128)(2,1)}, bf16[384,1408]{0,1:T(8,128)(2,1)}, bf16[3,384,16,88]{1,3,2,0:T(8,128)(2,1)}, ...), branch_computations={%region_13.14_spmd, %region_14.16_spmd} | conditional | flops 2363320320 | bytes 39649360 | solution.py:54
  103.2 1.1 broadcast.158.clone
  104.4 1.1 broadcast.160
  109.1 2.3 constant_dynamic-update-slice_fusion
  111.5 1.6 fusion.81
  113.1 14.5 %collective-permute-start.7 = (bf16[128,2816]{0,1:T(8,128)(2,1)S(1)}, bf16[128,2816]{0,1:T(8,128)(2,1)S(1)}, u32[]{:S(2)}, u32[]{:S(2)}) collective-permute-start(bf16[128,2816]{0,1:T(8,128)(2,1)S(1)} %get-tuple-element.292), channel_id=1, source_target_pairs={{0,1},{1,2},{2,3},{3,4},{4,5},{5,6},{6,7},{7,8},{8,9},{9,10},{10,1... | collective-permute-start | bytes 2162696 | tf_op jit(solution)/shard_map/ppermute | solution.py:38
  127.6 1.3 collective-permute-start.8
  128.9 1.3 collective-permute-start.10
  130.2 5.6 %collective-permute-start.9 = (f32[128,32]{0,1:T(8,128)S(1)}, f32[128,32]{0,1:T(8,128)S(1)}, u32[]{:S(2)}, u32[]{:S(2)}) collective-permute-start(f32[128,32]{0,1:T(8,128)S(1)} %get-tuple-element.298), channel_id=1, source_target_pairs={{0,1},{1,2},{2,3},{3,4},{4,5},{5,6},{6,7},{7,8},{8,9},{9,10},{10,1... | collective-permute-start | bytes 49160 | tf_op jit(solution)/shard_map/ppermute | solution.py:38
  135.8 0.8 collective-permute-done.9
  136.7 2.1 pad_maximum_fusion.4
  139.2 0.7 conditional.12
  139.9 8.4 %conditional.13 = (f32[80,1408]{1,0:T(8,128)}) conditional(s32[]{:T(128)} %convert_element_type.91, () %tuple.71, (f32[384,1]{0,1:T(1,128)S(1)}, bf16[384,1408]{0,1:T(8,128)(2,1)}, bf16[384,2816]{0,1:T(8,128)(2,1)S(1)}, bf16[1408,4224]{1,0:T(8,128)(2,1)}, f32[1,1408]{1,0:T(1,128)}, /*index=5*/f32[384,1408]{1,0:T(8,128)}, ...), branch_computations={%region_18.19_spmd, %region_19.21_spmd} | conditional | flops 5097455616 | bytes 36246600 | solution.py:54
  139.9 0.8 broadcast.165
  149.7 215.4 %all-reduce.4.cloned.1.call-done = f32[80,1408]{1,0:T(8,128)} async-done(((f32[80,1408]{1,0:T(8,128)}), f32[80,1408]{1,0:T(8,128)}) %all-reduce.4.cloned.1.call-update) | async-done | bytes 450576
  365.1 0.9 constant_dynamic-slice_fusion
  366.0 1.3 collective-permute-start.11
  367.3 4.7 collective-permute-done.11
  372.0 1.4 conditional.14
  372.0 1.4 convert_add_fusion
  373.5 10.2 %conditional.15 = (f32[1408,1408]{1,0:T(8,128)}) conditional(s32[]{:T(128)} %convert_element_type.90, (bf16[384,1408]{0,1:T(8,128)(2,1)}, bf16[384,1408]{1,0:T(8,128)(2,1)S(1)}) %tuple.140, (bf16[320,1408]{1,0:T(8,128)(2,1)}, f32[320,1408]{1,0:T(8,128)S(1)}) %tuple.78), branch_computations={%region_24.25_spmd, %region_25.26_spmd} | conditional | flops 7612661760 | bytes 10633224 | solution.py:278
  373.5 10.2 %fusion.85 = f32[1408,1408]{1,0:T(8,128)} fusion(bf16[320,1408]{1,0:T(8,128)(2,1)} %get-tuple-element.136, f32[320,1408]{1,0:T(8,128)S(1)} %get-tuple-element.137), kind=kOutput, calls=%fused_computation.134 | convolution fusion | flops 7612661760 | bytes 10633216 | tf_op jit(solution)/shard_map/cond/branch_1_fun/dot_general | solution.py:64
  383.7 103.3 %reduce-scatter.4.cloned.1.call-done = f32[88,1408]{1,0:T(8,128)} async-done(((f32[1408,1408]{1,0:T(8,128)}), f32[88,1408]{1,0:T(8,128)}) %reduce-scatter.4.cloned.1.call-update) | async-done | bytes 495632
  (46 shorter events, 2.5 us)
Async XLA Ops:
  6.5 358.6 %all-reduce.4.cloned.1.call-start = ((), (), s32[]{:S(2)}) async-start(), calls=%async_computation.1 | async-start | bytes 901120
  6.5 67.5 %copy-start.15 = (s32[384]{0:T(512)S(1)}, s32[384]{0:T(512)}, u32[]{:S(2)}) copy-start(s32[384]{0:T(512)} %param.27) | copy-start | bytes 4612
  6.5 67.6 %copy-start.16 = (s32[80]{0:T(128)S(1)}, s32[80]{0:T(128)}, u32[]{:S(2)}) copy-start(s32[80]{0:T(128)} %param.26) | copy-start | bytes 964
  36.5 3.1 copy-start.7
  46.5 2.8 collective-permute-start
  49.3 6.4 %collective-permute-start.1 = (bf16[5,1408]{1,0:T(8,128)(2,1)S(1)}, bf16[5,1408]{1,0:T(8,128)(2,1)S(1)}, u32[]{:S(2)}, u32[]{:S(2)}) collective-permute-start(bf16[5,1408]{1,0:T(8,128)(2,1)S(1)} %collective-permute-done), channel_id=1, source_target_pairs={{0,15},{1,0},{2,1},{3,2},{4,3},{5,4},{6,5},{7,6},{8,7},{9,8},{10,9... | collective-permute-start | bytes 42248 | tf_op jit(solution)/shard_map/ppermute | solution.py:18
  55.7 4.1 collective-permute-start.2
  59.9 4.5 collective-permute-start.3
  64.4 8.6 %collective-permute-start.4 = (bf16[40,1408]{1,0:T(8,128)(2,1)S(1)}, bf16[40,1408]{1,0:T(8,128)(2,1)S(1)}, u32[]{:S(2)}, u32[]{:S(2)}) collective-permute-start(bf16[40,1408]{1,0:T(8,128)(2,1)S(1)} %pad_maximum_fusion.7), channel_id=1, source_target_pairs={{0,8},{1,9},{2,10},{3,11},{4,12},{5,13},{6,14},{7,15},{8,0},{9,1},... | collective-permute-start | bytes 337928 | tf_op jit(solution)/shard_map/ppermute | solution.py:18
  78.6 1.3 copy-start.2
  83.8 6.6 %collective-permute-start.5 = (bf16[128,2816]{0,1:T(8,128)(2,1)}, bf16[128,2816]{0,1:T(8,128)(2,1)}, u32[]{:S(2)}, u32[]{:S(2)}) collective-permute-start(bf16[128,2816]{0,1:T(8,128)(2,1)} %get-tuple-element.296), channel_id=1, source_target_pairs={{0,1},{1,2},{2,3},{3,4},{4,5},{5,6},{6,7},{7,8},{8,9},{9,10},{10,1... | collective-permute-start | bytes 2162696 | tf_op jit(solution)/shard_map/ppermute | solution.py:38
  86.7 5.0 %collective-permute-start.6 = (bf16[128,2816]{0,1:T(8,128)(2,1)S(1)}, bf16[128,2816]{0,1:T(8,128)(2,1)}, u32[]{:S(2)}, u32[]{:S(2)}) collective-permute-start(bf16[128,2816]{0,1:T(8,128)(2,1)S(1)} %get-tuple-element.297), channel_id=1, source_target_pairs={{1,0},{2,1},{3,2},{4,3},{5,4},{6,5},{7,6},{8,7},{9,8},{10,9},{11,1... | collective-permute-start | bytes 2162696 | tf_op jit(solution)/shard_map/ppermute | solution.py:39
  95.4 1.7 copy-start
  111.5 25.2 %copy-start.1 = (bf16[384,2816]{0,1:T(8,128)(2,1)S(1)}, bf16[384,2816]{0,1:T(8,128)(2,1)}, u32[]{:S(2)}) copy-start(bf16[384,2816]{0,1:T(8,128)(2,1)} %constant_dynamic-update-slice_fusion) | copy-start | bytes 6488068
  113.1 23.6 %collective-permute-start.7 = (bf16[128,2816]{0,1:T(8,128)(2,1)S(1)}, bf16[128,2816]{0,1:T(8,128)(2,1)S(1)}, u32[]{:S(2)}, u32[]{:S(2)}) collective-permute-start(bf16[128,2816]{0,1:T(8,128)(2,1)S(1)} %get-tuple-element.292), channel_id=1, source_target_pairs={{0,1},{1,2},{2,3},{3,4},{4,5},{5,6},{6,7},{7,8},{8,9},{9,10},{10,1... | collective-permute-start | bytes 2162696 | tf_op jit(solution)/shard_map/ppermute | solution.py:38
  127.6 9.1 %collective-permute-start.8 = (bf16[128,2816]{0,1:T(8,128)(2,1)S(1)}, bf16[128,2816]{0,1:T(8,128)(2,1)S(1)}, u32[]{:S(2)}, u32[]{:S(2)}) collective-permute-start(bf16[128,2816]{0,1:T(8,128)(2,1)S(1)} %get-tuple-element.293), channel_id=1, source_target_pairs={{1,0},{2,1},{3,2},{4,3},{5,4},{6,5},{7,6},{8,7},{9,8},{10,9},{11,1... | collective-permute-start | bytes 2162696 | tf_op jit(solution)/shard_map/ppermute | solution.py:39
  128.9 6.9 %collective-permute-start.10 = (f32[128,32]{0,1:T(8,128)S(1)}, f32[128,32]{0,1:T(8,128)S(1)}, u32[]{:S(2)}, u32[]{:S(2)}) collective-permute-start(f32[128,32]{0,1:T(8,128)S(1)} %get-tuple-element.299), channel_id=1, source_target_pairs={{1,0},{2,1},{3,2},{4,3},{5,4},{6,5},{7,6},{8,7},{9,8},{10,9},{11,1... | collective-permute-start | bytes 49160 | tf_op jit(solution)/shard_map/ppermute | solution.py:39
  130.2 6.4 %collective-permute-start.9 = (f32[128,32]{0,1:T(8,128)S(1)}, f32[128,32]{0,1:T(8,128)S(1)}, u32[]{:S(2)}, u32[]{:S(2)}) collective-permute-start(f32[128,32]{0,1:T(8,128)S(1)} %get-tuple-element.298), channel_id=1, source_target_pairs={{0,1},{1,2},{2,3},{3,4},{4,5},{5,6},{6,7},{7,8},{8,9},{9,10},{10,1... | collective-permute-start | bytes 49160 | tf_op jit(solution)/shard_map/ppermute | solution.py:38
  136.6 2.6 copy-start.3
  139.9 8.5 %copy-start.17 = (u32[32]{0:T(128)S(1)}, u32[32]{0:T(128)}, u32[]{:S(2)}) copy-start(u32[32]{0:T(128)} %constant.122) | copy-start | bytes 388
  148.3 338.7 %reduce-scatter.4.cloned.1.call-start = ((), (), s32[]{:S(2)}) async-start(), calls=%async_computation.2 | async-start | bytes 8425472
  366.0 6.0 %collective-permute-start.11 = (f32[5,1408]{1,0:T(8,128)S(1)}, f32[5,1408]{1,0:T(8,128)S(1)}, u32[]{:S(2)}, u32[]{:S(2)}) collective-permute-start(f32[5,1408]{1,0:T(8,128)S(1)} %constant_dynamic-slice_fusion), channel_id=1, source_target_pairs={{16,0},{17,1},{18,2},{19,3},{20,4},{21,5},{22,6},{23,7},{24,8},{25... | collective-permute-start | bytes 84488 | tf_op jit(solution)/shard_map/ppermute | solution.py:28
  372.0 1.5 copy-start.5
Sparse Core Ops, SparseCore 0:
  148.5 216.5 all-reduce.3
  383.9 103.1 reduce-scatter.3
